TPU v7x, 128 devices: a whole 4x4x4 slice. The times are simulated.
128 devices in a mesh: tm: 8 (over z, core), space: 16 (over y, x).
Axes of the slice: x: 4, y: 4, z: 4, core: 2. Of those that a mesh axis runs over, the one named last changes fastest.
Arguments:
- init_field: float32 [2, 128, 1024], P(None, 'space'), may hold values from -3 to 3
- guess: float32 [256, 2, 128, 1024], P('tm', None, 'space'), may hold values from -3 to 3
- slab_blocks: int32 [8], replicated, may hold values from 1 to 4, 16 in all
Outputs:
- updated: float32 [256, 2, 128, 1024], P('tm', None, 'space')
Inputs may be any that keep to these rules, and one draw needn't show every extreme that they name: slab_blocks sums to 16; some slab holds exactly 4.
All inputs are finite; a program needn't handle non-finite values.
Results may differ from a plain program's by a relative error of at most 0.000028.
Values sent between devices are 32-bit elements; how exact they have to be, the bound alone decides.
No kernel may reach another device: no remote copies, remote signals or barrier semaphores. Data moves between devices by JAX's collectives and lax.ppermute only.
A program may use at most 128 MiB of HBM per device.

v0:
```python
import jax
import jax.numpy as jnp
from jax import lax
from jax.sharding import PartitionSpec as P

diffusion_rate = (0.0035, 0.028, 0.224)
advection_rate = (0.003, 0.024, 0.192)


def padded(cells, sides, width):
    for axis, dim in sides:
        count = lax.axis_size(axis)
        ends = count - 1
        head = lax.slice_in_dim(cells, 0, width, axis=dim)
        tail = lax.slice_in_dim(cells, cells.shape[dim] - width, cells.shape[dim], axis=dim)
        cells = jnp.concatenate(
            [
                lax.ppermute(tail, axis, [(i, (i + 1) % count) for i in range(ends)]),
                cells,
                lax.ppermute(head, axis, [((i + 1) % count, i) for i in range(ends)]),
            ],
            axis=dim,
        )
    return cells


def passed_along(block, axis, distance):
    devices = range(lax.axis_size(axis))
    route = [(i - distance, i) for i in devices if i - distance in devices]
    return lax.ppermute(block, axis, route)


def burgers_step(extended, diffusion, advection):
    centre = extended[:, :, 1:-1]
    above_rows = extended[:, :, 2:]
    below_rows = extended[:, :, :-2]
    eastward = jnp.roll(centre, -1, axis=-1)
    westward = jnp.roll(centre, 1, axis=-1)
    laplace = above_rows + below_rows + eastward + westward - 4.0 * centre
    grad_x = eastward - westward
    grad_y = above_rows - below_rows
    return (
        centre
        + diffusion * laplace
        - advection * (centre[:, 0:1] * grad_x + centre[:, 1:2] * grad_y)
    )


def advance(initial, forcing, number, level):
    diffusion = diffusion_rate[level]
    advection = advection_rate[level]
    current = initial
    for step_index in range(number):
        extended = padded(current, (("space", 2),), 1)
        current = burgers_step(extended, diffusion, advection)
        if forcing is not None:
            current = current + forcing[step_index]
    return current


def body(init_field, guess, slab_blocks):
    slab_index = lax.axis_index("tm")
    slab_count = lax.axis_size("tm")
    my_blocks = slab_blocks[slab_index]
    first_state = init_field[None]
    strip_rows = guess.shape[2]
    width_cols = guess.shape[3]
    block_cap = guess.shape[0] // 8

    def previous(points, number):
        last_point = lax.dynamic_slice_in_dim(points, number - 1, 1, 0)
        arrived = passed_along(last_point, "tm", 1)
        return jnp.where(slab_index == 0, first_state, arrived)

    def starting(points, number):
        return jnp.concatenate([previous(points, number), points[:-1]], 0)

    begin_one = starting(guess, 8 * my_blocks)
    relaxed = advance(begin_one, None, 7, 0)
    c_points = advance(relaxed, None, 1, 0)
    begin_two = starting(c_points, 8 * my_blocks)
    relaxed = advance(begin_two, None, 7, 0)
    residue = advance(relaxed, None, 1, 0) - c_points
    forcing_one = residue + c_points - advance(begin_two, None, 1, 1)
    level_one = c_points.reshape(block_cap, 8, 2, strip_rows, width_cols)
    forcing_grid = forcing_one.reshape(block_cap, 8, 2, strip_rows, width_cols)
    inner_forcing = jnp.moveaxis(forcing_grid[:, :7], 1, 0)
    heads = starting(level_one[:, 7], my_blocks)
    relaxed = advance(heads, inner_forcing, 7, 1)
    coarse_now = advance(relaxed, forcing_grid[:, 7][None], 1, 1)
    heads = starting(coarse_now, my_blocks)
    relaxed = advance(heads, inner_forcing, 7, 1)
    remainder = forcing_grid[:, 7] - coarse_now + advance(relaxed, None, 1, 1)
    forcing_two = remainder + coarse_now - advance(heads, None, 1, 2)

    def sweep_turn(turn_index, carry):
        incoming, kept = carry
        current = jnp.where(slab_index == 0, first_state, incoming)
        outputs = []
        for member in range(block_cap):
            advanced = advance(current, forcing_two[member][None, None], 1, 2)
            current = jnp.where(member < my_blocks, advanced, current)
            outputs.append(current[0])
        kept = jnp.where(turn_index == slab_index, jnp.stack(outputs, 0), kept)
        incoming = passed_along(current, "tm", 1)
        return (incoming, kept)

    empty_state = jnp.zeros_like(first_state)
    empty_kept = jnp.zeros_like(forcing_two)
    _, solved = lax.fori_loop(0, slab_count, sweep_turn, (empty_state, empty_kept))
    current = starting(solved, my_blocks)
    collected = []
    for member in range(7):
        current = advance(current, forcing_grid[:, member][None], 1, 1)
        collected.append(current)
    collected.append(solved)
    final = jnp.stack(collected, 1).reshape(guess.shape)
    live_rows = jnp.arange(guess.shape[0]) < 8 * my_blocks
    return jnp.where(live_rows[:, None, None, None], final, 0.0)


def solution(mesh):
    placed = (P(None, "space", None), P("tm", None, "space", None), P())
    return jax.shard_map(
        body, mesh=mesh, in_specs=placed, out_specs=P("tm", None, "space", None), check_vma=False
    )
```

profile of v0, /device:TPU:88, one launch (start us, length us, event | category | flops | bytes accessed | tf_op | source)
XLA Modules:
  0.0 890.2 jit_solution(10487335695098556505)
XLA Ops:
  8.9 4.8 collective-permute-start.10
  20.2 6.6 collective-permute-done.11
  32.1 3.9 collective-permute-start.13
  40.3 4.0 collective-permute-done.13
  49.4 3.9 collective-permute-start.15
  56.8 4.0 collective-permute-done.15
  66.1 3.9 collective-permute-start.17
  72.5 4.0 collective-permute-done.17
  81.7 4.1 collective-permute-start.19
  88.0 4.0 collective-permute-done.19
  97.3 3.9 collective-permute-start.21
  103.6 4.0 collective-permute-done.21
  112.8 3.9 collective-permute-start.23
  119.1 4.0 collective-permute-done.23
  134.7 4.0 collective-permute-done.25
  157.3 4.0 collective-permute-start.44
  167.7 6.0 collective-permute-start.29
  177.6 6.5 collective-permute-done.30
  195.6 4.0 collective-permute-done.32
  211.2 4.0 collective-permute-done.34
  220.4 4.3 collective-permute-start.36
  226.7 4.0 collective-permute-done.36
  242.3 4.0 collective-permute-done.38
  257.8 4.0 collective-permute-done.40
  267.1 3.9 collective-permute-start.42
  273.4 4.0 collective-permute-done.42
  278.1 5.5 fusion
  299.2 3.9 collective-permute-start.49
  310.5 3.9 collective-permute-start.51
  321.7 3.9 collective-permute-start.53
  333.0 4.1 collective-permute-start.55
  344.2 3.9 collective-permute-start.57
  355.5 3.9 collective-permute-start.59
  371.4 3.9 collective-permute-start.62
  427.2 4.0 collective-permute-done.72
  433.7 3.9 collective-permute-start.74
  452.5 357.8 %while.18 = (s32[]{:T(128)}, f32[1,2,8,1024]{3,2,1,0:T(8,128)S(1)}, f32[4,2,8,1024]{3,2,1,0:T(8,128)S(1)}, pred[]{:T(512)}, pred[]{:T(512)}, /*index=5*/pred[]{:...) while((s32[]{:T(128)}, f32[1,2,8,1024]{3,2,1,0:T(8,128)S(1)}, ...), condition=%wide.region_1.2_spmd.clone, body=%wide.region_0.1_spmd.clone.sunk | while | flops 1654788 | bytes 4850174 | solution.py:110
  499.2 3.9 collective-permute-start.1
  509.0 3.9 collective-permute-start.3
  528.6 3.9 collective-permute-start.7
  598.4 3.9 collective-permute-start.3
  608.2 3.9 collective-permute-start.5
  618.0 3.9 collective-permute-start.7
  697.7 3.9 collective-permute-start.5
  722.8 3.9 collective-permute-start.1
  828.3 3.9 collective-permute-start.81
  873.8 4.0 collective-permute-done.89
  880.2 3.9 collective-permute-start.91
  (673 shorter events, 685.2 us)
Async XLA Ops:
  8.9 11.3 %collective-permute-start.10 = (f32[32,2,1,1024]{3,2,1,0:T(1,128)S(1)}, f32[32,2,1,1024]{3,2,1,0:T(1,128)S(1)}, u32[]{:S(2)}, u32[]{:S(2)}) collective-permute-start(f32[32,2,1,1024]{3,2,1,0:T(1,128)S(1)} %get-tuple-element.422), channel_id=1, source_target_pairs={{1,0},{2,1},{3,2},{4,3},{5,4},{6,5},{7,6},{8,7},{9,8},{10,9},{11,1... | collective-permute-start | bytes 786440 | tf_op jit(solution)/shard_map/ppermute | solution.py:20
  13.7 13.1 %collective-permute-start.11 = (f32[32,2,1,1024]{3,2,1,0:T(1,128)S(1)}, f32[32,2,1,1024]{3,2,1,0:T(1,128)S(1)}, u32[]{:S(2)}, u32[]{:S(2)}) collective-permute-start(f32[32,2,1,1024]{3,2,1,0:T(1,128)S(1)} %get-tuple-element.421), channel_id=1, source_target_pairs={{0,1},{1,2},{2,3},{3,4},{4,5},{5,6},{6,7},{7,8},{8,9},{9,10},{10,1... | collective-permute-start | bytes 786440 | tf_op jit(solution)/shard_map/ppermute | solution.py:18
  30.1 10.1 %collective-permute-start.12 = (f32[32,2,1,1024]{3,2,1,0:T(1,128)S(1)}, f32[32,2,1,1024]{3,2,1,0:T(1,128)S(1)}, u32[]{:S(2)}, u32[]{:S(2)}) collective-permute-start(f32[32,2,1,1024]{3,2,1,0:T(1,128)S(1)} %get-tuple-element.414), channel_id=1, source_target_pairs={{1,0},{2,1},{3,2},{4,3},{5,4},{6,5},{7,6},{8,7},{9,8},{10,9},{11,1... | collective-permute-start | bytes 786440 | tf_op jit(solution)/shard_map/ppermute | solution.py:20
  32.1 12.2 %collective-permute-start.13 = (f32[32,2,1,1024]{3,2,1,0:T(1,128)S(1)}, f32[32,2,1,1024]{3,2,1,0:T(1,128)S(1)}, u32[]{:S(2)}, u32[]{:S(2)}) collective-permute-start(f32[32,2,1,1024]{3,2,1,0:T(1,128)S(1)} %get-tuple-element.413), channel_id=1, source_target_pairs={{0,1},{1,2},{2,3},{3,4},{4,5},{5,6},{6,7},{7,8},{8,9},{9,10},{10,1... | collective-permute-start | bytes 786440 | tf_op jit(solution)/shard_map/ppermute | solution.py:18
  47.5 9.3 %collective-permute-start.14 = (f32[32,2,1,1024]{3,2,1,0:T(1,128)S(1)}, f32[32,2,1,1024]{3,2,1,0:T(1,128)S(1)}, u32[]{:S(2)}, u32[]{:S(2)}) collective-permute-start(f32[32,2,1,1024]{3,2,1,0:T(1,128)S(1)} %get-tuple-element.406), channel_id=1, source_target_pairs={{1,0},{2,1},{3,2},{4,3},{5,4},{6,5},{7,6},{8,7},{9,8},{10,9},{11,1... | collective-permute-start | bytes 786440 | tf_op jit(solution)/shard_map/ppermute | solution.py:20
  49.4 11.4 %collective-permute-start.15 = (f32[32,2,1,1024]{3,2,1,0:T(1,128)S(1)}, f32[32,2,1,1024]{3,2,1,0:T(1,128)S(1)}, u32[]{:S(2)}, u32[]{:S(2)}) collective-permute-start(f32[32,2,1,1024]{3,2,1,0:T(1,128)S(1)} %get-tuple-element.405), channel_id=1, source_target_pairs={{0,1},{1,2},{2,3},{3,4},{4,5},{5,6},{6,7},{7,8},{8,9},{9,10},{10,1... | collective-permute-start | bytes 786440 | tf_op jit(solution)/shard_map/ppermute | solution.py:18
  64.1 8.4 collective-permute-start.16
  66.1 10.5 %collective-permute-start.17 = (f32[32,2,1,1024]{3,2,1,0:T(1,128)S(1)}, f32[32,2,1,1024]{3,2,1,0:T(1,128)S(1)}, u32[]{:S(2)}, u32[]{:S(2)}) collective-permute-start(f32[32,2,1,1024]{3,2,1,0:T(1,128)S(1)} %get-tuple-element.397), channel_id=1, source_target_pairs={{0,1},{1,2},{2,3},{3,4},{4,5},{5,6},{6,7},{7,8},{8,9},{9,10},{10,1... | collective-permute-start | bytes 786440 | tf_op jit(solution)/shard_map/ppermute | solution.py:18
  79.7 8.3 collective-permute-start.18
  81.7 10.4 %collective-permute-start.19 = (f32[32,2,1,1024]{3,2,1,0:T(1,128)S(1)}, f32[32,2,1,1024]{3,2,1,0:T(1,128)S(1)}, u32[]{:S(2)}, u32[]{:S(2)}) collective-permute-start(f32[32,2,1,1024]{3,2,1,0:T(1,128)S(1)} %get-tuple-element.389), channel_id=1, source_target_pairs={{0,1},{1,2},{2,3},{3,4},{4,5},{5,6},{6,7},{7,8},{8,9},{9,10},{10,1... | collective-permute-start | bytes 786440 | tf_op jit(solution)/shard_map/ppermute | solution.py:18
  95.3 8.3 collective-permute-start.20
  97.3 10.4 %collective-permute-start.21 = (f32[32,2,1,1024]{3,2,1,0:T(1,128)S(1)}, f32[32,2,1,1024]{3,2,1,0:T(1,128)S(1)}, u32[]{:S(2)}, u32[]{:S(2)}) collective-permute-start(f32[32,2,1,1024]{3,2,1,0:T(1,128)S(1)} %get-tuple-element.381), channel_id=1, source_target_pairs={{0,1},{1,2},{2,3},{3,4},{4,5},{5,6},{6,7},{7,8},{8,9},{9,10},{10,1... | collective-permute-start | bytes 786440 | tf_op jit(solution)/shard_map/ppermute | solution.py:18
  110.9 8.3 collective-permute-start.22
  112.8 10.4 %collective-permute-start.23 = (f32[32,2,1,1024]{3,2,1,0:T(1,128)S(1)}, f32[32,2,1,1024]{3,2,1,0:T(1,128)S(1)}, u32[]{:S(2)}, u32[]{:S(2)}) collective-permute-start(f32[32,2,1,1024]{3,2,1,0:T(1,128)S(1)} %get-tuple-element.373), channel_id=1, source_target_pairs={{0,1},{1,2},{2,3},{3,4},{4,5},{5,6},{6,7},{7,8},{8,9},{9,10},{10,1... | collective-permute-start | bytes 786440 | tf_op jit(solution)/shard_map/ppermute | solution.py:18
  126.5 8.3 collective-permute-start.24
  128.4 10.4 %collective-permute-start.25 = (f32[32,2,1,1024]{3,2,1,0:T(1,128)S(1)}, f32[32,2,1,1024]{3,2,1,0:T(1,128)S(1)}, u32[]{:S(2)}, u32[]{:S(2)}) collective-permute-start(f32[32,2,1,1024]{3,2,1,0:T(1,128)S(1)} %get-tuple-element.365), channel_id=1, source_target_pairs={{0,1},{1,2},{2,3},{3,4},{4,5},{5,6},{6,7},{7,8},{8,9},{9,10},{10,1... | collective-permute-start | bytes 786440 | tf_op jit(solution)/shard_map/ppermute | solution.py:18
  151.4 12.9 %collective-permute-start.27 = (f32[32,2,1,1024]{3,2,1,0:T(1,128)S(1)}, f32[32,2,1,1024]{3,2,1,0:T(1,128)S(1)}, u32[]{:S(2)}, u32[]{:S(2)}) collective-permute-start(f32[32,2,1,1024]{3,2,1,0:T(1,128)S(1)} %get-tuple-element.357), channel_id=1, source_target_pairs={{1,0},{2,1},{3,2},{4,3},{5,4},{6,5},{7,6},{8,7},{9,8},{10,9},{11,1... | collective-permute-start | bytes 786440 | tf_op jit(solution)/shard_map/ppermute | solution.py:20
  153.3 11.0 %collective-permute-start.28 = (f32[32,2,1,1024]{3,2,1,0:T(1,128)S(1)}, f32[32,2,1,1024]{3,2,1,0:T(1,128)S(1)}, u32[]{:S(2)}, u32[]{:S(2)}) collective-permute-start(f32[32,2,1,1024]{3,2,1,0:T(1,128)S(1)} %get-tuple-element.358), channel_id=1, source_target_pairs={{0,1},{1,2},{2,3},{3,4},{4,5},{5,6},{6,7},{7,8},{8,9},{9,10},{10,1... | collective-permute-start | bytes 786440 | tf_op jit(solution)/shard_map/ppermute | solution.py:18
  157.3 126.6 %collective-permute-start.44 = (f32[4,2,1,1024]{3,2,1,0:T(1,128)}, f32[4,2,1,1024]{3,2,1,0:T(1,128)}, u32[]{:S(2)}, u32[]{:S(2)}) collective-permute-start(f32[4,2,1,1024]{3,2,1,0:T(1,128)} %get-tuple-element.606), channel_id=1, source_target_pairs={{1,0},{2,1},{3,2},{4,3},{5,4},{6,5},{7,6},{8,7},{9,8},{10,9},{11,1... | collective-permute-start | bytes 98312 | tf_op jit(solution)/shard_map/ppermute | solution.py:20
  161.3 122.6 %collective-permute-start.45 = (f32[4,2,1,1024]{3,2,1,0:T(1,128)S(1)}, f32[4,2,1,1024]{3,2,1,0:T(1,128)}, u32[]{:S(2)}, u32[]{:S(2)}) collective-permute-start(f32[4,2,1,1024]{3,2,1,0:T(1,128)S(1)} %get-tuple-element.605), channel_id=1, source_target_pairs={{0,1},{1,2},{2,3},{3,4},{4,5},{5,6},{6,7},{7,8},{8,9},{9,10},{10,1... | collective-permute-start | bytes 98312 | tf_op jit(solution)/shard_map/ppermute | solution.py:18
  167.7 9.9 %collective-permute-start.29 = (f32[32,2,1,1024]{3,2,1,0:T(1,128)S(1)}, f32[32,2,1,1024]{3,2,1,0:T(1,128)S(1)}, u32[]{:S(2)}, u32[]{:S(2)}) collective-permute-start(f32[32,2,1,1024]{3,2,1,0:T(1,128)S(1)} %get-tuple-element.350), channel_id=1, source_target_pairs={{1,0},{2,1},{3,2},{4,3},{5,4},{6,5},{7,6},{8,7},{9,8},{10,9},{11,1... | collective-permute-start | bytes 786440 | tf_op jit(solution)/shard_map/ppermute | solution.py:20
  173.7 10.4 %collective-permute-start.30 = (f32[32,2,1,1024]{3,2,1,0:T(1,128)S(1)}, f32[32,2,1,1024]{3,2,1,0:T(1,128)S(1)}, u32[]{:S(2)}, u32[]{:S(2)}) collective-permute-start(f32[32,2,1,1024]{3,2,1,0:T(1,128)S(1)} %get-tuple-element.349), channel_id=1, source_target_pairs={{0,1},{1,2},{2,3},{3,4},{4,5},{5,6},{6,7},{7,8},{8,9},{9,10},{10,1... | collective-permute-start | bytes 786440 | tf_op jit(solution)/shard_map/ppermute | solution.py:18
  187.3 8.3 collective-permute-start.31
  189.3 10.4 %collective-permute-start.32 = (f32[32,2,1,1024]{3,2,1,0:T(1,128)S(1)}, f32[32,2,1,1024]{3,2,1,0:T(1,128)S(1)}, u32[]{:S(2)}, u32[]{:S(2)}) collective-permute-start(f32[32,2,1,1024]{3,2,1,0:T(1,128)S(1)} %get-tuple-element.341), channel_id=1, source_target_pairs={{0,1},{1,2},{2,3},{3,4},{4,5},{5,6},{6,7},{7,8},{8,9},{9,10},{10,1... | collective-permute-start | bytes 786440 | tf_op jit(solution)/shard_map/ppermute | solution.py:18
  202.9 8.3 collective-permute-start.33
  204.9 10.4 %collective-permute-start.34 = (f32[32,2,1,1024]{3,2,1,0:T(1,128)S(1)}, f32[32,2,1,1024]{3,2,1,0:T(1,128)S(1)}, u32[]{:S(2)}, u32[]{:S(2)}) collective-permute-start(f32[32,2,1,1024]{3,2,1,0:T(1,128)S(1)} %get-tuple-element.333), channel_id=1, source_target_pairs={{0,1},{1,2},{2,3},{3,4},{4,5},{5,6},{6,7},{7,8},{8,9},{9,10},{10,1... | collective-permute-start | bytes 786440 | tf_op jit(solution)/shard_map/ppermute | solution.py:18
  218.4 8.3 collective-permute-start.35
  220.4 10.4 %collective-permute-start.36 = (f32[32,2,1,1024]{3,2,1,0:T(1,128)S(1)}, f32[32,2,1,1024]{3,2,1,0:T(1,128)S(1)}, u32[]{:S(2)}, u32[]{:S(2)}) collective-permute-start(f32[32,2,1,1024]{3,2,1,0:T(1,128)S(1)} %get-tuple-element.325), channel_id=1, source_target_pairs={{0,1},{1,2},{2,3},{3,4},{4,5},{5,6},{6,7},{7,8},{8,9},{9,10},{10,1... | collective-permute-start | bytes 786440 | tf_op jit(solution)/shard_map/ppermute | solution.py:18
  234.0 8.3 collective-permute-start.37
  236.0 10.4 %collective-permute-start.38 = (f32[32,2,1,1024]{3,2,1,0:T(1,128)S(1)}, f32[32,2,1,1024]{3,2,1,0:T(1,128)S(1)}, u32[]{:S(2)}, u32[]{:S(2)}) collective-permute-start(f32[32,2,1,1024]{3,2,1,0:T(1,128)S(1)} %get-tuple-element.317), channel_id=1, source_target_pairs={{0,1},{1,2},{2,3},{3,4},{4,5},{5,6},{6,7},{7,8},{8,9},{9,10},{10,1... | collective-permute-start | bytes 786440 | tf_op jit(solution)/shard_map/ppermute | solution.py:18
  249.5 8.3 collective-permute-start.39
  251.5 10.4 %collective-permute-start.40 = (f32[32,2,1,1024]{3,2,1,0:T(1,128)S(1)}, f32[32,2,1,1024]{3,2,1,0:T(1,128)S(1)}, u32[]{:S(2)}, u32[]{:S(2)}) collective-permute-start(f32[32,2,1,1024]{3,2,1,0:T(1,128)S(1)} %get-tuple-element.309), channel_id=1, source_target_pairs={{0,1},{1,2},{2,3},{3,4},{4,5},{5,6},{6,7},{7,8},{8,9},{9,10},{10,1... | collective-permute-start | bytes 786440 | tf_op jit(solution)/shard_map/ppermute | solution.py:18
  265.1 8.3 collective-permute-start.41
  267.1 10.4 %collective-permute-start.42 = (f32[32,2,1,1024]{3,2,1,0:T(1,128)S(1)}, f32[32,2,1,1024]{3,2,1,0:T(1,128)S(1)}, u32[]{:S(2)}, u32[]{:S(2)}) collective-permute-start(f32[32,2,1,1024]{3,2,1,0:T(1,128)S(1)} %get-tuple-element.301), channel_id=1, source_target_pairs={{0,1},{1,2},{2,3},{3,4},{4,5},{5,6},{6,7},{7,8},{8,9},{9,10},{10,1... | collective-permute-start | bytes 786440 | tf_op jit(solution)/shard_map/ppermute | solution.py:18
  299.2 7.9 collective-permute-start.49
  310.5 7.9 collective-permute-start.51
  321.7 7.9 collective-permute-start.53
  333.0 7.9 collective-permute-start.55
  344.2 7.9 collective-permute-start.57
  355.5 7.9 collective-permute-start.59
  371.4 7.9 collective-permute-start.62
  381.8 7.9 collective-permute-start.64
  392.1 7.9 collective-permute-start.66
  402.4 7.9 collective-permute-start.68
  412.7 7.9 collective-permute-start.70
  423.0 8.2 collective-permute-start.72
  433.7 7.9 collective-permute-start.74
  869.5 8.2 collective-permute-start.89
  (115 other events, 742.0 us)
where the time goes:
time: 903 us; the launch traced here: 890 us
  starting transfers between devices  444 us (49%)
  waiting for transfers between devices  339 us (38%)
  other arithmetic  60.8 us (7%)
  local copies, waits for them, and re-layouts  38.4 us (4%)
    ppermute x71, starting transfers between devices, padded(): lax.ppermute(tail, axis, [(i, (i + 1) % count) for i in range(ends)])  273 us
    ppermute x71, waiting for transfers between devices, padded(): lax.ppermute(tail, axis, [(i, (i + 1) % count) for i in range(ends)])  268 us
    ppermute x71, starting transfers between devices, padded(): lax.ppermute(head, axis, [((i + 1) % count, i) for i in range(ends)])  145 us
    ppermute x13, waiting for transfers between devices, passed_along(): return lax.ppermute(block, axis, route)  37.2 us
    ppermute x71, waiting for transfers between devices, padded(): lax.ppermute(head, axis, [((i + 1) % count, i) for i in range(ends)])  34.2 us
    sub x15, other arithmetic, burgers_step(): centre + diffusion * laplace  31.4 us
    ppermute x13, starting transfers between devices, passed_along(): return lax.ppermute(block, axis, route)  24.9 us
    slice x132, local copies, waits for them, and re-layouts, burgers_step(): eastward = jnp.roll(centre, -1, axis=-1)  22.8 us
  transfers between devices with their start and end apart: 155, of which 99 were waited for; matrix products, arithmetic and copies ran while one was open for 5% of the time, Pallas kernels for 0%

commit v1 on v0

v1 whole, which is shorter than its diff:
```python
import jax
import jax.numpy as jnp
from jax import lax
from jax.experimental import pallas as pl
from jax.experimental.pallas import tpu as pltpu
from jax.sharding import PartitionSpec as P

diffusion_rate = (0.0035, 0.028, 0.224)
advection_rate = (0.003, 0.024, 0.192)
F32 = jnp.float32

SNAKE = [4 * (s // 4) + (s % 4 if (s // 4) % 2 == 0 else 3 - s % 4) for s in range(16)]
SMEM = pl.BlockSpec(memory_space=pltpu.SMEM)
VMEM = pl.BlockSpec(memory_space=pltpu.VMEM)
SINGLE = (2, 16, 8, 128)
QUAD = (2, 4, 16, 8, 128)


def shape(*dims):
    return jax.ShapeDtypeStruct(dims, F32)


def whole(kernel, outs, inputs, vregs, scratch=()):
    return pl.pallas_call(
        kernel,
        out_shape=outs,
        in_specs=[SMEM] + [VMEM] * inputs,
        out_specs=jax.tree.map(lambda _: VMEM, outs),
        scratch_shapes=list(scratch),
        compiler_params=pltpu.CompilerParams(vmem_limit_bytes=32 * 1024 * 1024),
        cost_estimate=pl.CostEstimate(flops=11 * 1024 * vregs, bytes_accessed=512 * vregs, transcendentals=0),
        name=kernel.__name__,
    )


def lanes():
    return lax.broadcasted_iota(jnp.int32, (8, 128), 1)


def picked(u, index):
    return jnp.take_along_axis(u, index, axis=1, mode="promise_in_bounds")


def exchanged(tiles, sizes):
    tiles, lane = list(tiles), lanes()
    apart = len(tiles) // 2
    for size in sizes:
        lower = (lane // size) % 2 == 0
        for a in range(len(tiles)):
            if (a // apart) % 2 == 0:
                x, y = tiles[a], tiles[a + apart]
                tiles[a] = jnp.where(lower, x, pltpu.roll(y, size, 1))
                tiles[a + apart] = jnp.where(lower, pltpu.roll(x, 128 - size, 1), y)
        apart //= 2
    return tiles


def quad_order():
    lane = lanes()
    return 4 * (lane % 32) + lane // 32


def single_order():
    lane = lanes()
    return 32 * (lane % 4) + lane // 4


def step(p, q, level):
    d = diffusion_rate[level]
    sub = lax.broadcasted_iota(jnp.int32, (8, 128), 0)
    wp, ep, sq, nq = d + p, d - p, d + q, d - q

    def one(u):
        after_last = jnp.where(sub == 7, 0.0, pltpu.roll(u[0], 7, 0))
        before_first = jnp.where(sub == 0, 0.0, pltpu.roll(u[15], 1, 0))
        north = jnp.concatenate([u[1:], after_last[None]], 0)
        south = jnp.concatenate([before_first[None], u[:-1]], 0)
        east = pltpu.roll(u, 127, 2)
        west = pltpu.roll(u, 1, 2)
        return (1.0 - 4.0 * d) * u + ep * east + wp * west + nq * north + sq * south

    return one(p), one(q)


def quad_step(read, write, level):
    d = diffusion_rate[level]
    sub = lax.broadcasted_iota(jnp.int32, (8, 128), 0)

    def row(k):
        return [[read(c, j, k) for j in range(4)] for c in range(2)]

    first = row(0)
    south = [[jnp.where(sub == 0, 0.0, pltpu.roll(u, 1, 0)) for u in us] for us in row(15)]
    beyond = [[jnp.where(sub == 7, 0.0, pltpu.roll(u, 7, 0)) for u in us] for us in first]
    here = first
    for k in range(16):
        north = row(k + 1) if k < 15 else beyond
        edge_east = [pltpu.roll(us[0], 127, 1) for us in here]
        edge_west = [pltpu.roll(us[3], 1, 1) for us in here]
        for j in range(4):
            p, q = here[0][j], here[1][j]
            wp, ep, sq, nq = d + p, d - p, d + q, d - q
            made = []
            for c in range(2):
                east = here[c][j + 1] if j < 3 else edge_east[c]
                west = here[c][j - 1] if j > 0 else edge_west[c]
                made.append(
                    ((1.0 - 4.0 * d) * here[c][j] + ep * east)
                    + (wp * west + nq * north[c][j])
                    + sq * south[c][j]
                )
            write(j, k, *made)
        south, here = here, north


def reader(ref, *lead):
    return lambda c, j, k: ref[(*lead, c, j, k)]


def writer(ref, *lead):
    def write(j, k, p, q):
        ref[(*lead, 0, j, k)] = p
        ref[(*lead, 1, j, k)] = q

    return write


def adder(ref, g, t):
    def write(j, k, p, q):
        ref[0, j, k] = p + g[t, 0, j, k]
        ref[1, j, k] = q + g[t, 1, j, k]

    return write


def eight_fine_steps(a, b):
    @pl.loop(0, 4)
    def _(_):
        quad_step(reader(a), writer(b), 0)
        quad_step(reader(b), writer(a), 0)


def eight_forced_steps(a, b, g):
    @pl.loop(0, 4)
    def _(n):
        quad_step(reader(a), adder(b, g, 2 * n), 1)
        quad_step(reader(b), adder(a, g, 2 * n + 1), 1)


def vectors():
    return [(c, j, k) for c in range(2) for j in range(4) for k in range(16)]


def tail_kernel(slab_blocks, guess, init, out):
    slab = lax.axis_index("tm")
    last = 8 * slab_blocks[slab] - 1
    out[0] = guess[last - 1]
    out[1] = jnp.where(slab == 7, init[...], guess[last])


def windows_kernel(slab_blocks, guess, before, out):
    lane = lanes()
    column = quad_order()
    even_from, odd_from = (column + 96) % 128, (column + 32) % 128
    even_cut, odd_cut = column < 32, column < 96

    @pl.loop(0, 16)
    def _(n):
        t, c = n // 2, n % 2
        evens, odds = [], []
        for i in range(4):
            rows = guess[jnp.maximum(8 * i + t - 2, 0), c]
            if i == 0:
                rows = jnp.where(t < 2, before[jnp.minimum(t, 1), c], rows)
            rows = advection_rate[0] * rows
            tiles = [rows[:, 128 * n : 128 * n + 128] for n in range(8)]
            a = [picked(u, even_from) for u in tiles]
            b = [picked(u, odd_from) for u in tiles]
            evens.append([jnp.where(even_cut, a[n - 1], a[n]) for n in range(8)])
            odds.append([jnp.where(odd_cut, b[n], b[(n + 1) % 8]) for n in range(8)])
        for n in range(8):
            for s, made in ((2 * n, evens), (2 * n + 1, odds)):
                for j, u in enumerate(exchanged([made[i][n] for i in range(4)], (64, 32))):
                    out[SNAKE[s], t, c, j] = u


def fine_kernel(slab_blocks, points, g, v, last, init, a, b):
    slab = lax.axis_index("tm")
    lane = lanes()
    flat = points.reshape(16 * 8 * 2 * 4 * 8, 128)

    def taken(t, c, j, k):
        return flat[pl.ds((k // 8) * 512 + t * 64 + c * 32 + j * 8 + k % 8, 8, stride=1024), :]

    @pl.loop(0, 8)
    def _(t):
        for c, j, k in vectors():
            a[c, j, k] = taken(t, c, j, k)
        eight_fine_steps(a, b)

        @pl.when(t == 0)
        def _():
            start = (lane < 32) & (slab == 0)
            for c, j, k in vectors():
                a[c, j, k] = jnp.where(start, taken(1, c, j, k), a[c, j, k])
                v[c, j, k] = 8.0 * a[c, j, k]

        quad_step(lambda c, j, k: 8.0 * a[c, j, k], writer(g, t), 1)
        eight_fine_steps(a, b)
        for c, j, k in vectors():
            g[t, c, j, k] = 8.0 * a[c, j, k] - g[t, c, j, k]

    for c in range(2):
        for k in range(16):
            u = 8.0 * taken(1, c, 0, k)
            for j in range(1, 4):
                u = jnp.where(lane // 32 == j, pltpu.roll(8.0 * taken(1, c, j, k), 32 * j, 1), u)
            init[c, k] = u

    eight_forced_steps(v, b, g)
    shift = 128 - 32 * (slab_blocks[slab] - 1)
    for c in range(2):
        for k in range(16):
            u = pltpu.roll(v[c, 0, k], shift % 128, 1)
            for j in range(1, 4):
                u = jnp.where(lane // 32 == j, pltpu.roll(v[c, j, k], (shift + 32 * j) % 128, 1), u)
            last[c, k] = u


def second_pass_kernel(slab_blocks, v, arrived, init, g, big, left, right, a, b, coarse):
    slab = lax.axis_index("tm")
    lane = lanes()
    for c in range(2):
        for k in range(16):
            before = jnp.where(slab == 0, init[c, k], arrived[c, k])
            for j in range(4):
                head = before if j == 0 else pltpu.roll(before, 128 - 32 * j, 1)
                a[c, j, k] = jnp.where(lane < 32, head, pltpu.roll(v[c, j, k], 32, 1))
    quad_step(lambda c, j, k: 8.0 * a[c, j, k], writer(coarse), 2)
    eight_forced_steps(a, b, g)
    order = single_order()
    blocks = slab_blocks[slab]
    for c in range(2):
        for k in range(16):
            made = exchanged([8.0 * a[c, j, k] - coarse[c, j, k] for j in range(4)], (64, 32))
            made = [jnp.where(i < blocks, picked(made[i], order), 0.0) for i in range(4)]
            to_left, to_right = pltpu.roll(made[0], 96, 1), pltpu.roll(made[0], 64, 1)
            for i in range(4):
                big[i, c, k] = made[i]
                if i:
                    to_left = jnp.where(lane // 32 == i, pltpu.roll(made[i], (32 * i + 96) % 128, 1), to_left)
                    to_right = jnp.where(lane // 32 == i, pltpu.roll(made[i], (32 * i + 64) % 128, 1), to_right)
            left[c, k] = to_left
            right[c, k] = to_right


def merge_kernel(
    slab_blocks, mine, mine_left, mine_right, mine_init, other, other_left, other_right, other_init, big, init
):
    lane = lanes()
    order = single_order()
    odd = lax.axis_index("tm") % 2
    for slot, centre, lower, upper in (
        (odd, mine, mine_left, mine_right),
        (1 - odd, other, other_left, other_right),
    ):
        for c in range(2):
            for k in range(16):
                low, high = lower[c, k], upper[c, k]
                for i in range(4):
                    u = jnp.where(lane < 32, pltpu.roll(low, (128 - 32 * i) % 128, 1) if i else low, centre[i, c, k])
                    u = jnp.where(lane >= 96, pltpu.roll(high, 96 - 32 * i, 1) if i < 3 else high, u)
                    big[4 * slot + i, c, k] = u
    for c in range(2):
        for k in range(16):
            init[c, k] = 8.0 * picked(jnp.where(odd == 1, other_init[c, k], mine_init[c, k]), order)


def coarse_steps(p, q, big, first, number):
    def turn(i, s):
        a, b = step(s[0], s[1], 2)
        return a + big[i, 0], b + big[i, 1]

    return lax.fori_loop(first, first + number, turn, (p, q))


def sweep_kernel(slab_blocks, state, big, out):
    even = lax.axis_index("tm") // 2 * 2
    p, q = coarse_steps(state[0], state[1], big, 0, slab_blocks[even])
    p, q = coarse_steps(p, q, big, 4, slab_blocks[even + 1])
    out[0] = p
    out[1] = q


def last_pass_kernel(slab_blocks, state, big, g, out, solved, a, b):
    slab = lax.axis_index("tm")
    odd = slab % 2
    lane = lanes()
    order = quad_order()
    flat = out.reshape(16 * 8 * 4 * 8, 128)
    scale = 1.0 / advection_rate[1]
    first_half = lane % 32 < 16

    def put(t, j, k, p, q):
        u = jnp.where(first_half, pltpu.roll(p, 120, 1), pltpu.roll(q, 8, 1))
        flat[pl.ds((k // 8) * 256 + t * 32 + j * 8 + k % 8, 8, stride=512), :] = scale * u

    p, q = coarse_steps(state[0], state[1], big, 0, odd * slab_blocks[slab - odd])
    for i in range(4):
        solved[i, 0] = p
        solved[i, 1] = q
        p, q = step(p, q, 2)
        p, q = p + big[4 * odd + i, 0], q + big[4 * odd + i, 1]
    solved[4, 0] = p
    solved[4, 1] = q

    for k in range(16):
        heads = [
            exchanged([0.125 * picked(solved[i, c, k], order) for i in range(4)], (64, 32)) for c in range(2)
        ]
        ends = [
            exchanged([0.125 * picked(solved[i + 1, c, k], order) for i in range(4)], (64, 32)) for c in range(2)
        ]
        for j in range(4):
            a[0, j, k] = heads[0][j]
            a[1, j, k] = heads[1][j]
            put(7, j, k, ends[0][j], ends[1][j])

    def forced(ref, t):
        def write(j, k, p, q):
            p, q = p + g[t, 0, j, k], q + g[t, 1, j, k]
            ref[0, j, k] = p
            ref[1, j, k] = q
            put(t, j, k, p, q)

        return write

    @pl.loop(0, 3)
    def _(n):
        quad_step(reader(a), forced(b, 2 * n), 1)
        quad_step(reader(b), forced(a, 2 * n + 1), 1)

    quad_step(reader(a), forced(b, 6), 1)


def strips_kernel(slab_blocks, packed, out):
    lane = lanes()
    blocks = slab_blocks[lax.axis_index("tm")]
    order = lane // 64 * 64 + 16 * (lane % 4) + lane % 64 // 4

    @pl.loop(0, 8)
    def _(t):
        for n in range(8):
            made = exchanged([packed[SNAKE[2 * n + h], t, j] for h in range(2) for j in range(4)], (64, 32, 16))
            for i in range(4):
                for c in range(2):
                    u = jnp.where(i < blocks, picked(made[2 * i + c], order), 0.0)
                    out[8 * i + t, c, :, 128 * n : 128 * n + 128] = u


def body(init_field, guess, slab_blocks):
    ring = [(k, (k + 1) % 8) for k in range(8)]
    cores = [(k, k ^ 1) for k in range(8)]
    up = [(SNAKE[s], SNAKE[(s + 1) % 16]) for s in range(16)]
    down = [(SNAKE[(s + 1) % 16], SNAKE[s]) for s in range(16)]
    quad_scratch = pltpu.VMEM(QUAD, F32)

    with jax.named_scope("column_windows"):
        tail = whole(tail_kernel, shape(2, 2, 8, 1024), 2, 32)(slab_blocks, guess, init_field)
        before = lax.ppermute(tail, "tm", ring)
        pieces = whole(windows_kernel, shape(16, 8, 2, 4, 8, 128), 2, 1024)(slab_blocks, guess, before)
        points = lax.all_to_all(pieces, "space", 0, 0, tiled=True)

    with jax.named_scope("fine_and_first_pass"):
        g, v, last, init1 = whole(
            fine_kernel,
            (shape(8, *QUAD), shape(*QUAD), shape(*SINGLE), shape(*SINGLE)),
            1,
            1024 * 18,
            (quad_scratch, quad_scratch),
        )(slab_blocks, points)
        arrived = lax.ppermute(last, "tm", ring)

    with jax.named_scope("second_pass"):
        big, left, right = whole(
            second_pass_kernel,
            (shape(4, *SINGLE), shape(*SINGLE), shape(*SINGLE)),
            4,
            128 * 10,
            (quad_scratch, quad_scratch, quad_scratch),
        )(slab_blocks, v, arrived, init1, g)

    with jax.named_scope("coarsest_level"):
        upper = lax.ppermute(left, "space", down)
        lower = lax.ppermute(right, "space", up)
        others = [lax.ppermute(x, "tm", cores) for x in (big, lower, upper, init1)]
        full, state = whole(merge_kernel, (shape(8, *SINGLE), shape(*SINGLE)), 8, 512)(
            slab_blocks, big, lower, upper, init1, *others
        )
        plane = lax.axis_index("tm") // 2
        for turn in range(3):
            sent = whole(sweep_kernel, shape(*SINGLE), 2, 32 * 8)(slab_blocks, state, full)
            route = [(2 * turn + core, 2 * turn + 2 + core) for core in range(2)]
            came = lax.ppermute(sent, "tm", route)
            state = jnp.where(plane == turn + 1, came, state)

    with jax.named_scope("last_pass"):
        packed = whole(
            last_pass_kernel,
            shape(16, 8, 4, 8, 128),
            3,
            128 * 10,
            (pltpu.VMEM((5, *SINGLE), F32), quad_scratch, quad_scratch),
        )(slab_blocks, state, full, g)
        packed = lax.all_to_all(packed, "space", 0, 0, tiled=True)
        return whole(strips_kernel, shape(*guess.shape), 1, 512)(slab_blocks, packed)


def solution(mesh):
    placed = (P(None, "space", None), P("tm", None, "space", None), P())
    return jax.shard_map(
        body, mesh=mesh, in_specs=placed, out_specs=P("tm", None, "space", None), check_vma=False
    )
```

time: 903 us -> 204 us (0.23)
  the two profiles are of different devices: /device:TPU:88 before, /device:TPU:96 now
where the time goes in v1:
time: 204 us
  blocking collectives  86.8 us (43%)
  Pallas kernels  75.8 us (37%)
  waiting for transfers between devices  29.2 us (14%)
  starting transfers between devices  6.57 us (3%)
  local copies, waits for them, and re-layouts  5.28 us (3%)
    all_to_all x1, blocking collectives, body(): points = lax.all_to_all(pieces, 'space', 0, 0, tiled=True)  55.3 us
    pallas_call x1, Pallas kernels, body(): whole(fine_kernel, (shape(8, *QUAD), shape(*QUAD), shape(*SINGLE), shape(...  33.9 us
    all_to_all x1, blocking collectives, body(): packed = lax.all_to_all(packed, 'space', 0, 0, tiled=True)  31.5 us
    pallas_call x1, Pallas kernels, body(): whole(last_pass_kernel, shape(16, 8, 4, 8, 128), 3, 128 * 10, (pltpu.VMEM...  15.9 us
    ppermute x3, waiting for transfers between devices, body(): came = lax.ppermute(sent, 'tm', route)  15.7 us
    pallas_call x1, Pallas kernels, body(): whole(windows_kernel, shape(16, 8, 2, 4, 8, 128), 2, 1024)  7.28 us
    pallas_call x1, Pallas kernels, body(): whole(second_pass_kernel, (shape(4, *SINGLE), shape(*SINGLE), shape(*SING...  6.99 us
    pallas_call x1, Pallas kernels, body(): whole(strips_kernel, shape(*guess.shape), 1, 512)(slab_blocks, packed)  6.55 us
  transfers between devices with their start and end apart: 11, of which 6 were waited for; matrix products, arithmetic and copies ran while one was open for 0% of the time, Pallas kernels for 0%

profile of v1, /device:TPU:96, one launch (start us, length us, event | category | flops | bytes accessed | tf_op | source)
XLA Modules:
  0.0 204.0 jit_solution(10977498544591023080)
XLA Ops:
  0.0 0.0 copy-start.2
  0.0 1.6 copy-done.2
  1.6 0.0 copy-start.3
  1.6 0.8 copy-done.3
  2.4 0.0 copy-start.4
  2.4 0.7 copy-done.4
  3.1 0.6 tail_kernel.1
  3.7 0.0 collective-permute-start
  3.7 4.4 %collective-permute-done.before = f32[2,2,8,1024]{3,2,1,0:T(8,128)S(1)} collective-permute-done((f32[2,2,8,1024]{3,2,1,0:T(8,128)S(1)}, f32[2,2,8,1024]{3,2,1,0:T(8,128)S(1)}, u32[]{:S(2)}, u32[]{:S(2)}) %collective-permute-start) | collective-permute-done | bytes 131104 | tf_op jit(solution)/shard_map/column_windows/ppermute | solution.py:370
  8.1 7.3 %windows_kernel.1 = f32[16,8,2,4,8,128]{5,4,3,2,1,0:T(8,128)S(1)} custom-call(s32[8]{0:T(128)S(1)} %copy-done.4, f32[32,2,8,1024]{3,2,1,0:T(8,128)S(1)} %copy-done.2, f32[2,2,8,1024]{3,2,1,0:T(8,128)S(1)} %collective-permute-done.before), custom_call_target="tpu_custom_call" | custom-call | flops 11534336 | bytes 524288 | tf_op jit(solution)/shard_map/column_windows/windows_kernel/pallas_call | solution.py:371
  15.4 55.3 %all_to_all.10.points = f32[16,8,2,4,8,128]{5,4,3,2,1,0:T(8,128)S(1)} all-to-all(f32[16,8,2,4,8,128]{5,4,3,2,1,0:T(8,128)S(1)} %windows_kernel.1), channel_id=1, replica_groups=mesh['tm'=8,'space'=16] {'space'}, dimensions={0} | all-to-all | bytes 8388608 | tf_op jit(solution)/shard_map/column_windows/all_to_all | solution.py:372
  70.7 33.9 %fine_kernel.1 = (f32[8,2,4,16,8,128]{5,4,3,2,1,0:T(8,128)S(1)}, f32[2,4,16,8,128]{4,3,2,1,0:T(8,128)S(1)}, f32[2,16,8,128]{3,2,1,0:T(8,128)S(1)}, f32[2,16,8,128]{3,2,1,0:T(8,128)S(1)}) custom-call(s32[8]{0:T(128)S(1)} %copy-done.4, f32[16,8,2,4,8,128]{5,4,3,2,1,0:T(8,128)S(1)} %all_to_all.10.points), custom_call_target="tpu_custom_call" | custom-call | flops 207618048 | bytes 9437184 | tf_op jit(solution)/shard_map/fine_and_first_pass/fine_kernel/pallas_call | solution.py:375
  104.6 0.0 copy-start
  104.6 0.0 collective-permute-start.1
  104.6 4.4 %collective-permute-done.1.arrived = f32[2,16,8,128]{3,2,1,0:T(8,128)S(1)} collective-permute-done((f32[2,16,8,128]{3,2,1,0:T(8,128)S(1)}, f32[2,16,8,128]{3,2,1,0:T(8,128)S(1)}, u32[]{:S(2)}, u32[]{:S(2)}) %collective-permute-start.1) | collective-permute-done | bytes 131104 | tf_op jit(solution)/shard_map/fine_and_first_pass/ppermute | solution.py:382
  109.0 7.0 %second_pass_kernel.1 = (f32[4,2,16,8,128]{4,3,2,1,0:T(8,128)S(1)}, f32[2,16,8,128]{3,2,1,0:T(8,128)S(1)}, f32[2,16,8,128]{3,2,1,0:T(8,128)S(1)}) custom-call(s32[8]{0:T(128)S(1)} %copy-done.4, f32[2,4,16,8,128]{4,3,2,1,0:T(8,128)S(1)} %get-tuple-element.14.v, f32[2,16,8,128]{3,2,1,0:T(8,128)S(1)} %collective-permute-done.1.arrived, ...), custom_call_target="tpu_custom_call" | custom-call | flops 14417920 | bytes 655360 | tf_op jit(solution)/shard_map/second_pass/second_pass_kernel/pallas_call | solution.py:385
  116.0 0.0 copy-done
  116.0 0.0 copy-start.5
  116.0 0.1 collective-permute-start.4
  116.1 0.7 collective-permute-start.2
  116.8 2.6 %collective-permute-start.3 = (f32[2,16,8,128]{3,2,1,0:T(8,128)S(1)}, f32[2,16,8,128]{3,2,1,0:T(8,128)S(1)}, u32[]{:S(2)}, u32[]{:S(2)}) collective-permute-start(f32[2,16,8,128]{3,2,1,0:T(8,128)S(1)} %get-tuple-element.20), channel_id=1, source_target_pairs={{1,0},{2,1},{3,2},{7,3},{6,7},{5,6},{4,5},{8,4},{9,8},{10,9},{11,1... | collective-permute-start | bytes 393224 | tf_op jit(solution)/shard_map/coarsest_level/ppermute | solution.py:394
  119.4 0.0 collective-permute-start.7
  119.4 3.8 %collective-permute-done.2.mine_left = f32[2,16,8,128]{3,2,1,0:T(8,128)S(1)} collective-permute-done((f32[2,16,8,128]{3,2,1,0:T(8,128)S(1)}, f32[2,16,8,128]{3,2,1,0:T(8,128)S(1)}, u32[]{:S(2)}, u32[]{:S(2)}) %collective-permute-start.2) | collective-permute-done | bytes 131104 | tf_op jit(solution)/shard_map/coarsest_level/ppermute | solution.py:395
  123.2 0.0 collective-permute-start.5
  123.2 0.0 collective-permute-done.3.mine_right
  123.2 0.5 collective-permute-start.6
  123.7 0.0 collective-permute-done.7.other_init
  123.7 0.8 collective-permute-done.5.other_left
  124.6 0.2 collective-permute-done.6.other_right
  124.8 0.0 collective-permute-done.4.other
  124.8 1.0 merge_kernel.1
  125.8 1.2 sweep_kernel.3
  127.0 0.7 collective-permute-start.8
  127.7 0.0 collective-permute-done.8
  127.7 0.0 copy-done.5
  127.7 1.2 sweep_kernel.4
  128.9 0.7 collective-permute-start.9
  129.6 0.0 collective-permute-done.9
  129.7 1.2 sweep_kernel.5
  130.9 1.3 collective-permute-start.10
  132.2 15.6 %collective-permute-done.10 = f32[2,16,8,128]{3,2,1,0:T(8,128)S(1)} collective-permute-done((f32[2,16,8,128]{3,2,1,0:T(8,128)S(1)}, f32[2,16,8,128]{3,2,1,0:T(8,128)S(1)}, u32[]{:S(2)}, u32[]{:S(2)}) %collective-permute-start.10) | collective-permute-done | bytes 131104 | tf_op jit(solution)/shard_map/coarsest_level/ppermute | solution.py:404
  147.8 0.0 copy-start.1
  147.8 2.2 %copy-done.1 = f32[8,2,4,16,8,128]{5,4,3,2,1,0:T(8,128)S(1)} copy-done((f32[8,2,4,16,8,128]{5,4,3,2,1,0:T(8,128)S(1)}, f32[8,2,4,16,8,128]{5,4,3,2,1,0:T(8,128)}, u32[]{:S(2)}) %copy-start.1) | copy-done | bytes 4194328
  150.0 15.9 %last_pass_kernel.1 = f32[16,8,4,8,128]{4,3,2,1,0:T(8,128)S(1)} custom-call(s32[8]{0:T(128)S(1)} %copy-done.5, f32[2,16,8,128]{3,2,1,0:T(8,128)S(1)} %broadcast_select_fusion.2.state, f32[8,2,16,8,128]{4,3,2,1,0:T(8,128)S(1)} %get-tuple-element.22.big, f32[8,2,4,16,8,128]{5,4,3,2,1,0:T(8,128)S(1)} %copy-done.1), custom_call_target="tpu_custom_call" | custom-call | flops 14417920 | bytes 655360 | tf_op jit(solution)/shard_map/last_pass/last_pass_kernel/pallas_call | solution.py:408
  166.0 31.5 %all_to_all.11.packed = f32[16,8,4,8,128]{4,3,2,1,0:T(8,128)S(1)} all-to-all(f32[16,8,4,8,128]{4,3,2,1,0:T(8,128)S(1)} %last_pass_kernel.1), channel_id=1, replica_groups=mesh['tm'=8,'space'=16] {'space'}, dimensions={0} | all-to-all | bytes 4194304 | tf_op jit(solution)/shard_map/last_pass/all_to_all | solution.py:415
  197.5 6.5 %strips_kernel.1 = f32[32,2,8,1024]{3,2,1,0:T(8,128)} custom-call(s32[8]{0:T(128)S(1)} %copy-done.5, f32[16,8,4,8,128]{4,3,2,1,0:T(8,128)S(1)} %all_to_all.11.packed), custom_call_target="tpu_custom_call" | custom-call | flops 5767168 | bytes 262144 | tf_op jit(solution)/shard_map/last_pass/strips_kernel/pallas_call | solution.py:416
  (3 shorter events, 0.1 us)
Async XLA Ops:
  0.0 1.6 copy-start.2
  1.6 0.8 copy-start.3
  2.4 0.7 copy-start.4
  3.7 4.4 %collective-permute-start = (f32[2,2,8,1024]{3,2,1,0:T(8,128)S(1)}, f32[2,2,8,1024]{3,2,1,0:T(8,128)S(1)}, u32[]{:S(2)}, u32[]{:S(2)}) collective-permute-start(f32[2,2,8,1024]{3,2,1,0:T(8,128)S(1)} %tail_kernel.1), channel_id=1, source_target_pairs={{0,16},{16,32},{32,48},{48,64},{64,80},{80,96},{96,112},{112,0},{1... | collective-permute-start | bytes 393224 | tf_op jit(solution)/shard_map/column_windows/ppermute | solution.py:370
  104.6 11.4 %copy-start = (f32[8,2,4,16,8,128]{5,4,3,2,1,0:T(8,128)}, f32[8,2,4,16,8,128]{5,4,3,2,1,0:T(8,128)S(1)}, u32[]{:S(2)}) copy-start(f32[8,2,4,16,8,128]{5,4,3,2,1,0:T(8,128)S(1)} %get-tuple-element.17.g) | copy-start | bytes 12582916
  104.6 4.4 %collective-permute-start.1 = (f32[2,16,8,128]{3,2,1,0:T(8,128)S(1)}, f32[2,16,8,128]{3,2,1,0:T(8,128)S(1)}, u32[]{:S(2)}, u32[]{:S(2)}) collective-permute-start(f32[2,16,8,128]{3,2,1,0:T(8,128)S(1)} %get-tuple-element.15), channel_id=1, source_target_pairs={{0,16},{16,32},{32,48},{48,64},{64,80},{80,96},{96,112},{112,0},{1... | collective-permute-start | bytes 393224 | tf_op jit(solution)/shard_map/fine_and_first_pass/ppermute | solution.py:382
  116.0 11.7 %copy-start.5 = (s32[8]{0:T(128)S(1)}, s32[8]{0:T(128)}, u32[]{:S(2)}) copy-start(s32[8]{0:T(128)} %slab_blocks.19) | copy-start | bytes 100
  116.0 8.8 %collective-permute-start.4 = (f32[4,2,16,8,128]{4,3,2,1,0:T(8,128)S(1)}, f32[4,2,16,8,128]{4,3,2,1,0:T(8,128)S(1)}, u32[]{:S(2)}, u32[]{:S(2)}) collective-permute-start(f32[4,2,16,8,128]{4,3,2,1,0:T(8,128)S(1)} %get-tuple-element.18.mine), channel_id=1, source_target_pairs={{0,16},{16,0},{32,48},{48,32},{64,80},{80,64},{96,112},{112,96},{1... | collective-permute-start | bytes 1572872 | tf_op jit(solution)/shard_map/coarsest_level/ppermute | solution.py:396
  116.1 7.1 %collective-permute-start.2 = (f32[2,16,8,128]{3,2,1,0:T(8,128)S(1)}, f32[2,16,8,128]{3,2,1,0:T(8,128)S(1)}, u32[]{:S(2)}, u32[]{:S(2)}) collective-permute-start(f32[2,16,8,128]{3,2,1,0:T(8,128)S(1)} %get-tuple-element.19), channel_id=1, source_target_pairs={{0,1},{1,2},{2,3},{3,7},{7,6},{6,5},{5,4},{4,8},{8,9},{9,10},{10,1... | collective-permute-start | bytes 393224 | tf_op jit(solution)/shard_map/coarsest_level/ppermute | solution.py:395
  116.8 6.5 %collective-permute-start.3 = (f32[2,16,8,128]{3,2,1,0:T(8,128)S(1)}, f32[2,16,8,128]{3,2,1,0:T(8,128)S(1)}, u32[]{:S(2)}, u32[]{:S(2)}) collective-permute-start(f32[2,16,8,128]{3,2,1,0:T(8,128)S(1)} %get-tuple-element.20), channel_id=1, source_target_pairs={{1,0},{2,1},{3,2},{7,3},{6,7},{5,6},{4,5},{8,4},{9,8},{10,9},{11,1... | collective-permute-start | bytes 393224 | tf_op jit(solution)/shard_map/coarsest_level/ppermute | solution.py:394
  119.4 4.3 %collective-permute-start.7 = (f32[2,16,8,128]{3,2,1,0:T(8,128)S(1)}, f32[2,16,8,128]{3,2,1,0:T(8,128)S(1)}, u32[]{:S(2)}, u32[]{:S(2)}) collective-permute-start(f32[2,16,8,128]{3,2,1,0:T(8,128)S(1)} %get-tuple-element.16.init.mine_init), channel_id=1, source_target_pairs={{0,16},{16,0},{32,48},{48,32},{64,80},{80,64},{96,112},{112,96},{1... | collective-permute-start | bytes 393224 | tf_op jit(solution)/shard_map/coarsest_level/ppermute | solution.py:396
  123.2 1.3 collective-permute-start.5
  123.2 1.5 collective-permute-start.6
  127.0 0.7 collective-permute-start.8
  128.9 0.7 collective-permute-start.9
  130.9 16.9 %collective-permute-start.10 = (f32[2,16,8,128]{3,2,1,0:T(8,128)S(1)}, f32[2,16,8,128]{3,2,1,0:T(8,128)S(1)}, u32[]{:S(2)}, u32[]{:S(2)}) collective-permute-start(f32[2,16,8,128]{3,2,1,0:T(8,128)S(1)} %sweep_kernel.5), channel_id=1, source_target_pairs={{64,96},{80,112},{65,97},{81,113},{66,98},{82,114},{67,99},{83,115... | collective-permute-start | bytes 393224 | tf_op jit(solution)/shard_map/coarsest_level/ppermute | solution.py:404
  147.8 2.2 %copy-start.1 = (f32[8,2,4,16,8,128]{5,4,3,2,1,0:T(8,128)S(1)}, f32[8,2,4,16,8,128]{5,4,3,2,1,0:T(8,128)}, u32[]{:S(2)}) copy-start(f32[8,2,4,16,8,128]{5,4,3,2,1,0:T(8,128)} %copy-done) | copy-start | bytes 12582916
